TPU v7x, 32 devices: a whole 2x2x4 slice. The times are simulated.
32 devices in a mesh: grp: 2 (over y), seq: 4 (over z), wt: 2 (over x), head: 2 (over core).
Axes of the slice: x: 2, y: 2, z: 4, core: 2. Of those that a mesh axis runs over, the one named last changes fastest.
Arguments:
- hidden: bfloat16 [2048, 2048], P(('grp', 'seq', 'wt'), 'head'), parts along dimension 0, may hold values from -6 to 6
- norm_gain: float32 [2048], replicated, may hold values from 0.1 to 1.9
- w_proj_x: bfloat16 [2048, 4096], P('wt', 'head'), may hold values from -0.125 to 0.125
- w_proj_bc: bfloat16 [2048, 512], P('wt', 'head'), may hold values from -0.125 to 0.125
- w_proj_dt: bfloat16 [2048, 32], P('wt', 'head'), may hold values from -0.125 to 0.125
- dt_bias: float32 [32], P('head'), may hold values from -4 to -1
- a_log: float32 [32], P('head'), may hold values from -20 to 1
- d_skip: float32 [32], P('head'), may hold values from 0.5 to 1.5
- inner_gain: float32 [4096], P('head'), may hold values from 0.1 to 1.9
- w_out: bfloat16 [4096, 2048], P('head', 'wt'), may hold values from -0.09375 to 0.09375
- lengths: int32 [16], P(('grp', 'seq', 'wt')), parts along dimension 0, may hold values from 1 to 128, 768 in all
- mix_index: int32 [16, 4], P(('grp', 'seq', 'wt')), parts along dimension 0, may hold values from 0 to 7, as said below
- mix_gain: float32 [16, 4], P(('grp', 'seq', 'wt')), parts along dimension 0, may hold values from -0.5 to 0.5
Outputs:
- layer_out: bfloat16 [2048, 2048], P(('grp', 'seq', 'wt'), 'head'), parts along dimension 0
There are 2 independent parts, one for each index of `grp`. A program takes and returns all parts, laid end to end along the dimension named above; an argument that names none is the same for every part. Nothing has to cross between parts.
Inputs may be any that keep to these rules, and one draw needn't show every extreme that they name: `mix_index`: each listed block belongs to the same shard of 128 positions as its row's block or to one of the two shards next to it.
All inputs are finite; a program needn't handle non-finite values. No bound on the sum of `lengths` on one device may be relied on, other than what follows from the above.
Results may differ from a plain program's by a relative error of at most 0.0065.
Values may be sent and summed in bfloat16 or wider, within the bound.
A program may use at most 320 MiB of HBM per device.

v0:
```python
import jax
import jax.numpy as jnp
from jax import lax
from jax.sharding import PartitionSpec as P

SPAN = 128
BLK = 128
eps_value = 1e-05
highest = lax.Precision.HIGHEST


def prefix(value, axis, join, neutral):
    count, mine = (lax.axis_size(axis), lax.axis_index(axis))
    pieces = jax.tree.map(lambda part: lax.all_gather(part, axis), value)
    total = jax.tree.map(
        lambda part, zero: jnp.full_like(part, 0) + jnp.asarray(zero, part.dtype), value, neutral
    )

    def turn(position, total):
        longer = join(total, jax.tree.map(lambda part: part[position], pieces))
        return jax.tree.map(lambda new, old: jnp.where(position < mine, new, old), longer, total)

    return lax.fori_loop(0, count - 1, turn, total)


def extended(cells, sides, width):
    for axis, dim in sides:
        count = lax.axis_size(axis)
        ends = count - 1
        head = lax.slice_in_dim(cells, 0, width, axis=dim)
        tail = lax.slice_in_dim(cells, cells.shape[dim] - width, cells.shape[dim], axis=dim)
        cells = jnp.concatenate(
            [
                lax.ppermute(tail, axis, [(i, (i + 1) % count) for i in range(ends)]),
                cells,
                lax.ppermute(head, axis, [((i + 1) % count, i) for i in range(ends)]),
            ],
            axis=dim,
        )
    return cells


def span_local(x_span, b_span, c_span, dt_span, log_span):
    cumulated = jnp.cumsum(log_span, axis=0)
    length = x_span.shape[0]
    rows_at = jnp.arange(length, dtype=jnp.int32)
    lower_part = rows_at[:, None] >= rows_at[None, :]
    difference = cumulated.T[:, :, None] - cumulated.T[:, None, :]
    decays = jnp.where(lower_part[None], jnp.exp(jnp.where(lower_part[None], difference, 0.0)), 0.0)
    scores = jnp.dot(c_span, b_span.T, precision=highest)
    weights = scores[None] * decays * dt_span.T[:, None, :]
    outputs = jnp.einsum("hts,shp->thp", weights, x_span, precision=highest)
    tail_decay = jnp.exp(cumulated[-1][None, :] - cumulated) * dt_span
    weighted_x = x_span * tail_decay[:, :, None]
    state_new = jnp.einsum("shp,sn->hpn", weighted_x, b_span, precision=highest)
    return (outputs, state_new, cumulated)


def from_state(c_span, cumulated, state_in):
    return (
        jnp.einsum("tn,hpn->thp", c_span, state_in, precision=highest)
        * jnp.exp(cumulated)[:, :, None]
    )


def combine(earlier, later):
    return (earlier[0] + later[0], jnp.exp(later[0])[:, None, None] * earlier[1] + later[1])


def body(
    hidden,
    norm_gain,
    w_proj_x,
    w_proj_bc,
    w_proj_dt,
    dt_bias,
    a_log,
    d_skip,
    inner_gain,
    w_out,
    lengths,
    mix_index,
    mix_gain,
):
    tokens_here = hidden.shape[0]
    half_width = hidden.shape[1]
    whole_input = lax.all_gather(hidden, "head", axis=1, tiled=True)
    floats = whole_input.astype(jnp.float32)
    normed = (
        floats
        * lax.rsqrt(jnp.mean(floats * floats, axis=-1, keepdims=True) + eps_value)
        * norm_gain
    ).astype(jnp.bfloat16)
    pieces = (
        lax.all_gather(w_proj_x, "wt", axis=0, tiled=True),
        lax.all_gather(w_proj_bc, "wt", axis=0, tiled=True),
        lax.all_gather(w_proj_dt, "wt", axis=0, tiled=True),
    )
    x_sum, bc_sum, dt_raw = tuple(
        (
            jnp.dot(normed, weight_piece, preferred_element_type=jnp.float32)
            for weight_piece in pieces
        )
    )
    heads_here = w_proj_dt.shape[1]
    state_size = w_proj_bc.shape[1] // 2
    head_size = w_proj_x.shape[1] // heads_here
    x_in = jax.nn.silu(x_sum).astype(jnp.bfloat16)
    bc_in = jax.nn.silu(bc_sum).astype(jnp.bfloat16)
    shard_at = lax.axis_index(("seq", "wt"))
    live_mask = (jnp.arange(tokens_here, dtype=jnp.int32) < lengths[0]).astype(jnp.float32)
    steps_dt = jax.nn.softplus(dt_raw + dt_bias) * live_mask[:, None]
    log_decay = -steps_dt * jnp.exp(a_log)
    spans = tokens_here // SPAN
    x_float = x_in.astype(jnp.float32).reshape(spans, SPAN, heads_here, head_size)
    b_float = bc_in[:, :state_size].astype(jnp.float32).reshape(spans, SPAN, state_size)
    c_float = bc_in[:, state_size:].astype(jnp.float32).reshape(spans, SPAN, state_size)
    dt_float = steps_dt.reshape(spans, SPAN, heads_here)
    log_float = log_decay.reshape(spans, SPAN, heads_here)
    outputs, fresh_states, cumulated = jax.vmap(span_local)(
        x_float, b_float, c_float, dt_float, log_float
    )
    running = jnp.zeros((heads_here, head_size, state_size), jnp.float32)
    before = jnp.zeros((heads_here,), jnp.float32)
    arriving = [running]
    decayed = [before]
    running = jnp.exp(cumulated[0, -1])[:, None, None] * running + fresh_states[0]
    before = cumulated[0, -1]
    identity_pair = (
        jnp.zeros((heads_here,), jnp.float32),
        jnp.zeros((heads_here, head_size, state_size), jnp.float32),
    )
    entering = prefix((before, running), ("seq", "wt"), combine, identity_pair)
    initial = entering[1]
    incoming = jnp.stack(arriving) + jnp.exp(jnp.stack(decayed))[:, :, None, None] * initial[None]
    outputs = outputs + jax.vmap(from_state)(c_float, cumulated, incoming)
    y_full = outputs.reshape(tokens_here, heads_here, head_size) + d_skip[
        None, :, None
    ] * x_float.reshape(tokens_here, heads_here, head_size)
    scaling = lax.rsqrt(jnp.mean(y_full * y_full, axis=-1, keepdims=True) + eps_value)
    y_norm = (
        (y_full * scaling * inner_gain.reshape(heads_here, head_size))
        .astype(jnp.bfloat16)
        .reshape(tokens_here, heads_here * head_size)
    )
    partial_out = jnp.dot(
        y_norm, lax.all_gather(w_out, "wt", axis=1, tiled=True), preferred_element_type=jnp.float32
    )
    head_total = lax.psum_scatter(partial_out, "head", scatter_dimension=1, tiled=True)
    own_part = hidden.astype(jnp.float32)
    mixed_in = (own_part + head_total).astype(jnp.bfloat16)
    widened = extended(mixed_in, ((("seq", "wt"), 0),), tokens_here)
    per_shard = tokens_here // BLK
    blocks = widened.reshape(3 * per_shard, BLK, half_width)
    relative = mix_index - (shard_at * per_shard - per_shard)
    summed_mix = mixed_in.astype(jnp.float32).reshape(per_shard, BLK, half_width)
    for member in range(mix_index.shape[1]):
        summed_mix = summed_mix + mix_gain[:, member][:, None, None] * jnp.take(
            blocks, relative[:, member], axis=0
        ).astype(jnp.float32)
    return summed_mix.reshape(tokens_here, half_width).astype(jnp.bfloat16)


def solution(mesh):
    in_specs = (
        P(("grp", "seq", "wt"), "head"),
        P(),
        P("wt", "head"),
        P("wt", "head"),
        P("wt", "head"),
        P("head"),
        P("head"),
        P("head"),
        P("head"),
        P("head", "wt"),
        P(("grp", "seq", "wt")),
        P(("grp", "seq", "wt"), None),
        P(("grp", "seq", "wt"), None),
    )
    out_specs = P(("grp", "seq", "wt"), "head")
    return jax.shard_map(body, mesh=mesh, in_specs=in_specs, out_specs=out_specs, check_vma=False)
```

profile of v0, /device:TPU:9, one launch (start us, length us, event | category | flops | bytes accessed | tf_op | source)
XLA Modules:
  0.0 417.1 jit_solution(728118675776157198)
XLA Ops:
  6.5 0.7 all-gather.9.cloned.1.call-update
  7.3 0.7 all-gather.7.cloned.1.call-update
  8.7 0.7 exp.58
  9.4 3.6 all_gather.25
  13.0 3.8 all_gather.22
  16.8 0.2 fusion.3
  17.0 1.0 fusion.39
  18.1 0.1 multiply_bitcast_fusion
  18.2 0.1 copy.23
  18.3 0.2 reduce_window_sum.13
  18.5 0.1 bitcast_exponential_fusion
  18.6 0.1 copy.28
  18.7 12.7 %all-gather.9.cloned.1.call-done = bf16[2048,256]{1,0:T(8,128)(2,1)} async-done(((bf16[1024,256]{1,0:T(8,128)(2,1)}), bf16[2048,256]{1,0:T(8,128)(2,1)}) %all-gather.9.cloned.1.call-update) | async-done | bytes 1048592 | tf_op jit(solution)/shard_map/all_gather | solution.py:96
  31.4 1.6 multiply_convert_fusion.1
  33.0 104.0 %all-gather.7.cloned.1.call-done = bf16[2048,2048]{1,0:T(8,128)(2,1)} async-done(((bf16[1024,2048]{1,0:T(8,128)(2,1)}), bf16[2048,2048]{1,0:T(8,128)(2,1)}) %all-gather.7.cloned.1.call-update) | async-done | bytes 8388624 | tf_op jit(solution)/shard_map/all_gather | solution.py:95
  137.0 0.3 mul.233
  137.3 5.3 %bitcast_multiply_fusion.1 = (f32[128,2048]{1,0:T(8,128)S(1)}, bf16[128,2048]{1,0:T(8,128)(2,1)S(1)}) fusion(f32[16,8,16,128]{3,2,1,0:T(8,128)S(1)} %bitcast.107, bf16[2048,2048]{1,0:T(8,128)(2,1)} %all-gather.7.cloned.1.call-done, bf16[128,2048]{1,0:T(8,128)(2,1)S(1)} %all_gather.22, f32[2048]{0:T(1024)S(1)} %copy-done.4, f32[128]{0:T(128)S(1)} %add_rsqrt_fusion.1), kind=kOutput, calls=%fused_computation.17 | convolution fusion | flops 1076625408 | bytes 11543040 | tf_op jit(solution)/shard_map/dot_general | solution.py:101
  142.6 0.3 copy.34
  142.9 1.6 convolution_add_fusion
  144.6 0.5 all-gather.11.cloned.1.call-update
  145.3 13.8 %all-gather = f32[8,1,16]{2,1,0:T(1,128)S(1)} all-gather(f32[1,1,16]{2,1,0:T(1,128)S(1)} %get-tuple-element.141), channel_id=2, replica_groups=mesh['grp'=2,'seq'=4,'wt'=2,'head'=2] {'seq','wt'}, dimensions={0}, use_global_device_ids=true | all-gather | bytes 576 | tf_op jit(solution)/shard_map/all_gather | solution.py:14
  159.2 0.1 fusion.35
  159.3 0.2 copy.36
  159.5 0.3 copy.33
  159.8 107.6 %all-gather.13.cloned.1.call-done = f32[128,128,128]{2,1,0:T(8,128)} async-done(((f32[16,128,128]{2,1,0:T(8,128)}), f32[128,128,128]{2,1,0:T(8,128)}) %all-gather.13.cloned.1.call-update) | async-done | bytes 8388624 | tf_op jit(solution)/shard_map/all_gather | solution.py:14
  267.4 10.8 %while.15 = (s32[]{:T(128)}, f32[16,128,128]{2,1,0:T(8,128)S(1)}, s32[]{:T(128)}, f32[8,16]{1,0:T(8,128)S(1)}, f32[8,16,128,128]{3,2,1,0:T(8,128)}, /*index=5*/s32[]{:T(128)}, s32[]{:T(128)}) while((s32[]{:T(128)}, f32[16,128,128]{2,1,0:T(8,128)S(1)}, s32[]{:T(128)}, f32[8,16]{1,0:T(8,128)S(1)}, f32[8,16,128,128]{3,2,1,0:T(8,128)}, ...), condition=%wide.region_3.4_spmd.clone, body=%wide.region_2.3_spmd.clone.sunk | while | flops 1048580 | bytes 3146025 | solution.py:23
  267.4 1.5 fusion.62
  268.9 1.5 fusion.62
  270.4 1.5 fusion.62
  271.9 1.5 fusion.62
  273.4 1.5 fusion.62
  274.9 1.6 fusion.62
  276.6 1.6 fusion.62
  278.2 0.6 fusion.1
  278.8 2.6 fusion.9
  281.4 0.1 copy.32
  281.5 1.7 copy.35
  283.2 90.1 %all-gather.11.cloned.1.call-done = bf16[2048,2048]{1,0:T(8,128)(2,1)} async-done(((bf16[2048,1024]{1,0:T(8,128)(2,1)}), bf16[2048,2048]{1,0:T(8,128)(2,1)}) %all-gather.11.cloned.1.call-update) | async-done | bytes 8388624 | tf_op jit(solution)/shard_map/all_gather | solution.py:147
  373.3 0.3 mul.247
  373.7 6.1 %fusion.16 = f32[128,2048]{1,0:T(8,128)} fusion(bf16[2048,2048]{1,0:T(8,128)(2,1)} %all-gather.11.cloned.1.call-done, f32[16,8,16,128]{3,2,1,0:T(8,128)S(1)} %bitcast.101, f32[128,2048]{1,0:T(8,128)S(1)} %copy.35, f32[2048]{0:T(1024)S(1)} %copy-done.1, f32[2048]{0:T(1024)S(1)} %broadcast_bitcast_fusion, bf16[128,2048]{1,0:T(8,128)(2,1)S(1)} %get-tuple-element.153), kind=kOutput, calls=%fused_computation.29 | convolution fusion | flops 1075314688 | bytes 12075008 | tf_op jit(solution)/shard_map/dot_general | solution.py:146
  379.8 9.4 %reduce-scatter.2.cloned.1.call-done = f32[128,1024]{1,0:T(8,128)} async-done(((f32[128,2048]{1,0:T(8,128)}), f32[128,1024]{1,0:T(8,128)}) %reduce-scatter.2.cloned.1.call-update) | async-done | bytes 524304 | tf_op jit(solution)/shard_map/reduce_scatter | solution.py:149
  389.2 1.1 add_convert_fusion
  390.3 3.1 collective-permute-start
  393.4 3.1 collective-permute-start.1
  396.5 0.6 fusion.53
  404.6 0.7 fusion.52
  405.2 1.7 collective-permute-done.1
  407.0 3.6 fusion.31
  (39 shorter events, 0.6 us)
Async XLA Ops:
  6.5 130.8 %copy-start.4 = (f32[2048]{0:T(1024)S(1)}, f32[2048]{0:T(1024)}, u32[]{:S(2)}) copy-start(f32[2048]{0:T(1024)} %param.18) | copy-start | bytes 24580
  6.5 24.9 %all-gather.9.cloned.1.call-start = ((), (), s32[]{:S(2)}) async-start(), calls=%async_computation.2 | async-start | bytes 1572864 | tf_op jit(solution)/shard_map/all_gather | solution.py:96
  7.3 129.7 %all-gather.7.cloned.1.call-start = ((), (), s32[]{:S(2)}) async-start(), calls=%async_computation.1 | async-start | bytes 12582912 | tf_op jit(solution)/shard_map/all_gather | solution.py:95
  8.0 259.4 %all-gather.13.cloned.1.call-start = ((), (), s32[]{:S(2)}) async-start(), calls=%async_computation.5 | async-start | bytes 9437184 | tf_op jit(solution)/shard_map/all_gather | solution.py:14
  142.6 16.5 %copy-start.3 = (f32[16]{0:T(128)S(1)}, f32[16]{0:T(128)}, u32[]{:S(2)}) copy-start(f32[16]{0:T(128)} %param.24) | copy-start | bytes 196
  144.6 228.7 %all-gather.11.cloned.1.call-start = ((), (), s32[]{:S(2)}) async-start(), calls=%async_computation.3 | async-start | bytes 12582912 | tf_op jit(solution)/shard_map/all_gather | solution.py:147
  145.1 244.1 %reduce-scatter.2.cloned.1.call-start = ((), (), s32[]{:S(2)}) async-start(), calls=%async_computation.4 | async-start | bytes 1572864 | tf_op jit(solution)/shard_map/reduce_scatter | solution.py:149
  278.2 95.4 %copy-start.1 = (f32[2048]{0:T(1024)S(1)}, f32[2048]{0:T(1024)}, u32[]{:S(2)}) copy-start(f32[2048]{0:T(1024)} %param.25) | copy-start | bytes 24580
  373.6 15.6 %copy-start = (bf16[128,1024]{1,0:T(8,128)(2,1)S(1)}, bf16[128,1024]{1,0:T(8,128)(2,1)}, u32[]{:S(2)}) copy-start(bf16[128,1024]{1,0:T(8,128)(2,1)} %param.17) | copy-start | bytes 786436
  373.6 22.9 %copy-start.5 = (s32[1,4]{1,0:T(1,128)S(1)}, s32[1,4]{1,0:T(1,128)}, u32[]{:S(2)}) copy-start(s32[1,4]{1,0:T(1,128)} %param.28) | copy-start | bytes 52
  373.7 30.9 %copy-start.2 = (f32[1,4]{1,0:T(1,128)S(1)}, f32[1,4]{1,0:T(1,128)}, u32[]{:S(2)}) copy-start(f32[1,4]{1,0:T(1,128)} %param.29) | copy-start | bytes 52
  390.3 14.9 %collective-permute-start = (bf16[128,1024]{1,0:T(8,128)(2,1)S(1)}, bf16[128,1024]{1,0:T(8,128)(2,1)S(1)}, u32[]{:S(2)}, u32[]{:S(2)}) collective-permute-start(bf16[128,1024]{1,0:T(8,128)(2,1)S(1)} %add_convert_fusion), channel_id=1, source_target_pairs={{0,2},{2,4},{4,6},{6,8},{8,10},{10,12},{12,14},{1,3},{3,5},{5,7},{... | collective-permute-start | bytes 786440 | tf_op jit(solution)/shard_map/ppermute | solution.py:34
  393.4 13.5 %collective-permute-start.1 = (bf16[128,1024]{1,0:T(8,128)(2,1)S(1)}, bf16[128,1024]{1,0:T(8,128)(2,1)S(1)}, u32[]{:S(2)}, u32[]{:S(2)}) collective-permute-start(bf16[128,1024]{1,0:T(8,128)(2,1)S(1)} %add_convert_fusion), channel_id=1, source_target_pairs={{2,0},{4,2},{6,4},{8,6},{10,8},{12,10},{14,12},{3,1},{5,3},{7,5},{... | collective-permute-start | bytes 786440 | tf_op jit(solution)/shard_map/ppermute | solution.py:36
Sparse Core Ops, SparseCore 0:
  8.9 22.4 all-gather.8
  32.9 103.9 all-gather.6
  144.7 122.6 all-gather.12
  268.8 104.4 all-gather.10
  379.9 9.2 reduce-scatter.1
where the time goes:
time: 418 us; the launch traced here: 417 us
  waiting for transfers between devices  327 us (78%)
  between operations  21.4 us (5%)
  blocking collectives  21.3 us (5%)
  matrix products  18.9 us (5%)
  other arithmetic  15.8 us (4%)
  starting transfers between devices  6.34 us (2%)
  local copies, waits for them, and re-layouts  5.7 us (1%)
    all_gather x1, waiting for transfers between devices, prefix(): pieces = jax.tree.map(lambda part: lax.all_gather(part, axis), value)  108 us
    all_gather x1, waiting for transfers between devices, body(): lax.all_gather(w_proj_x, 'wt', axis=0, tiled=True)  104 us
    all_gather x1, waiting for transfers between devices, body(): lax.all_gather(w_out, 'wt', axis=1, tiled=True)  90.1 us
    all_gather x1, blocking collectives, prefix(): pieces = jax.tree.map(lambda part: lax.all_gather(part, axis), value)  13.8 us
    all_gather x1, waiting for transfers between devices, body(): lax.all_gather(w_proj_bc, 'wt', axis=0, tiled=True)  12.7 us
    select_n x7, other arithmetic, turn(): jnp.where(position < mine, new, old)  10.5 us
    reduce_scatter x1, waiting for transfers between devices, body(): lax.psum_scatter(partial_out, 'head', scatter_dimension=1, tiled=True)  9.42 us
  transfers between devices with their start and end apart: 7, of which 6 were waited for; matrix products, arithmetic and copies ran while one was open for 5% of the time, Pallas kernels for 0%

commit v1 on v0

--- a/solution.py
+++ b/solution.py
@@ -1,3 +1,4 @@
+import functools
 import jax
 import jax.numpy as jnp
 from jax import lax
@@ -7,6 +8,39 @@
 BLK = 128
 eps_value = 1e-05
 highest = lax.Precision.HIGHEST
+
+
+def set_desk_up(arr, which_dim):
+    arr = jnp.moveaxis(arr, 0, which_dim)
+    f_now = arr.shape
+    val2 = arr.reshape(
+        *f_now[:which_dim], f_now[which_dim] * f_now[which_dim + 1], *f_now[which_dim + 2 :]
+    )
+    return val2
+
+
+def enter_skins(w_in, mesh_dim):
+    w_next = lax.psum(1, mesh_dim)
+    extra = lax.axis_index(mesh_dim)
+    v_now, passed = (w_next, extra)
+    w2, block_out = (w_in[None], 1)
+    while block_out < v_now:
+        d_next = tuple(((at, at ^ block_out) for at in range(v_now)))
+        e_next = lax.ppermute(w2, mesh_dim, d_next)
+        known = passed & block_out == 0
+        small = jnp.where(known, w2, e_next)
+        n_now = jnp.where(known, e_next, w2)
+        w2 = jnp.concatenate([small, n_now])
+        block_out *= 2
+    return w2
+
+
+def _raise_heads(buf, values, dim_k):
+    p_next = set_desk_up(enter_skins(buf, values), dim_k)
+    return p_next
+
+
+expand_the_streams = functools.partial(_raise_heads, values="wt", dim_k=1)
 
 
 def prefix(value, axis, join, neutral):
@@ -143,9 +177,7 @@
         .astype(jnp.bfloat16)
         .reshape(tokens_here, heads_here * head_size)
     )
-    partial_out = jnp.dot(
-        y_norm, lax.all_gather(w_out, "wt", axis=1, tiled=True), preferred_element_type=jnp.float32
-    )
+    partial_out = jnp.dot(y_norm, expand_the_streams(w_out), preferred_element_type=jnp.float32)
     head_total = lax.psum_scatter(partial_out, "head", scatter_dimension=1, tiled=True)
     own_part = hidden.astype(jnp.float32)
     mixed_in = (own_part + head_total).astype(jnp.bfloat16)

time: 418 us -> 397 us (0.950)
  waiting for transfers between devices: 327 us -> 133 us
  blocking collectives: 21.3 us -> 163 us
  local copies, waits for them, and re-layouts: 5.7 us -> 20.8 us
  other arithmetic: 15.8 us -> 29.9 us
    all_gather x1, blocking collectives: 13.8 us -> 156 us  [prefix(): pieces = jax.tree.map(lambda part: lax.all_gather(part, axis), value)]
    all_gather x1, waiting for transfers between devices: 108 us -> 0.02 us  [prefix(): pieces = jax.tree.map(lambda part: lax.all_gather(part, axis), value)]
    all_gather x1 -> x0, waiting for transfers between devices: 90.1 us -> none  [body(): lax.all_gather(w_out, 'wt', axis=1, tiled=True)]
    exp x7, local copies, waits for them, and re-layouts: 0.06 us -> 8.77 us  [combine(): jnp.exp(later[0])[:, None, None] * earlier[1] + later[1]]
    concatenate x0 -> x1, other arithmetic: none -> 7.46 us  [enter_skins(): w2 = jnp.concatenate([small, n_now])]
    unnamed x12 -> x21, local copies, waits for them, and re-layouts: 0.04 us -> 6.56 us
    select_n x0 -> x1, other arithmetic: none -> 5.77 us  [enter_skins(): small = jnp.where(known, w2, e_next)]
  transfers between devices with their start and end apart: 7 -> 7, of which waited for: 6 -> 4; matrix products, arithmetic and copies ran while one was open for 5% -> 7% of each run, Pallas kernels for 0% -> 0%
where the time goes in v1:
time: 397 us; the launch traced here: 396 us
  blocking collectives  163 us (41%)
  waiting for transfers between devices  133 us (34%)
  other arithmetic  29.9 us (8%)
  between operations  21.8 us (5%)
  matrix products  20.9 us (5%)
  local copies, waits for them, and re-layouts  20.8 us (5%)
  starting transfers between devices  6.61 us (2%)
    all_gather x1, blocking collectives, prefix(): pieces = jax.tree.map(lambda part: lax.all_gather(part, axis), value)  156 us
    all_gather x1, waiting for transfers between devices, body(): lax.all_gather(w_proj_x, 'wt', axis=0, tiled=True)  104 us
    all_gather x1, waiting for transfers between devices, body(): lax.all_gather(w_proj_bc, 'wt', axis=0, tiled=True)  13.9 us
    reduce_scatter x1, waiting for transfers between devices, body(): lax.psum_scatter(partial_out, 'head', scatter_dimension=1, tiled=True)  12.3 us
    select_n x7, other arithmetic, turn(): jnp.where(position < mine, new, old)  10.2 us
    exp x7, local copies, waits for them, and re-layouts, combine(): jnp.exp(later[0])[:, None, None] * earlier[1] + later[1]  8.77 us
  transfers between devices with their start and end apart: 7, of which 4 were waited for; matrix products, arithmetic and copies ran while one was open for 7% of the time, Pallas kernels for 0%

profile of v1, /device:TPU:9, one launch (start us, length us, event | category | flops | bytes accessed | tf_op | source)
XLA Modules:
  0.0 396.2 jit_solution(16412527817980228813)
XLA Ops:
  6.6 0.7 all-gather.8.cloned.1.call-update
  7.3 0.7 all-gather.6.cloned.1.call-update
  8.8 3.4 all_gather.22
  12.2 3.6 all_gather.19
  16.0 0.3 fusion.39
  16.8 0.6 bitcast_exponential_fusion
  17.5 13.9 %all-gather.8.cloned.1.call-done = bf16[2048,256]{1,0:T(8,128)(2,1)} async-done(((bf16[1024,256]{1,0:T(8,128)(2,1)}), bf16[2048,256]{1,0:T(8,128)(2,1)}) %all-gather.8.cloned.1.call-update) | async-done | bytes 1048592 | tf_op jit(solution)/shard_map/all_gather | solution.py:130
  31.4 1.6 multiply_convert_fusion.1
  33.0 104.0 %all-gather.6.cloned.1.call-done = bf16[2048,2048]{1,0:T(8,128)(2,1)} async-done(((bf16[1024,2048]{1,0:T(8,128)(2,1)}), bf16[2048,2048]{1,0:T(8,128)(2,1)}) %all-gather.6.cloned.1.call-update) | async-done | bytes 8388624 | tf_op jit(solution)/shard_map/all_gather | solution.py:129
  137.0 0.3 mul.233
  137.3 5.3 %bitcast_multiply_fusion.1 = (f32[128,2048]{1,0:T(8,128)S(1)}, bf16[128,2048]{1,0:T(8,128)(2,1)S(1)}) fusion(f32[16,8,16,128]{3,2,1,0:T(8,128)S(1)} %bitcast.115, bf16[2048,2048]{1,0:T(8,128)(2,1)} %all-gather.6.cloned.1.call-done, bf16[128,2048]{1,0:T(8,128)(2,1)S(1)} %all_gather.19, f32[2048]{0:T(1024)S(1)} %copy-done.6, f32[128]{0:T(128)S(1)} %add_rsqrt_fusion.1), kind=kOutput, calls=%fused_computation.20 | convolution fusion | flops 1076625408 | bytes 11543040 | tf_op jit(solution)/shard_map/dot_general | solution.py:135
  142.6 0.3 copy.45
  143.0 1.7 convolution_add_fusion
  144.7 6.5 %copy.43 = bf16[2048,1024]{0,1:T(8,128)(2,1)} copy(bf16[2048,1024]{1,0:T(8,128)(2,1)} %param.26) | data formatting | bytes 8388608 | tf_op args[9]
  151.2 0.3 collective-permute-start
  151.6 156.2 %all-gather = f32[8,1,16]{2,1,0:T(1,128)} all-gather(f32[1,1,16]{2,1,0:T(1,128)S(1)} %get-tuple-element.143), channel_id=2, replica_groups=mesh['grp'=2,'seq'=4,'wt'=2,'head'=2] {'seq','wt'}, dimensions={0}, use_global_device_ids=true | all-gather | bytes 576 | tf_op jit(solution)/shard_map/all_gather | solution.py:48
  307.8 0.6 iota_compare_fusion
  308.4 0.7 broadcast_bitcast_fusion
  309.2 5.8 %broadcast_select_fusion.1 = (bf16[1,2048,1024]{1,2,0:T(8,128)(2,1)}, bf16[1,2048,1024]{1,2,0:T(8,128)(2,1)}) fusion(bf16[1,2048,1024]{1,2,0:T(8,128)(2,1)} %collective-permute-done, pred[]{:T(512)S(6)} %eq.3, bf16[2048,1024]{0,1:T(8,128)(2,1)} %copy.43), kind=kLoop, calls=%fused_computation.5 | loop fusion | flops 4194304 | bytes 16777216 | tf_op jit(solution)/shard_map/jit(_where)/select_n | solution.py:31
  315.0 7.5 %pad_maximum_fusion = bf16[2,2048,1024]{1,2,0:T(8,128)(2,1)} fusion(bf16[1,2048,1024]{1,2,0:T(8,128)(2,1)} %get-tuple-element.141, bf16[1,2048,1024]{1,2,0:T(8,128)(2,1)} %get-tuple-element.140), kind=kLoop, calls=%fused_computation.3 | loop fusion | flops 4194304 | bytes 16777216 | tf_op jit(solution)/shard_map/concatenate | solution.py:33
  323.0 19.1 %while.15 = (s32[]{:T(128)}, f32[16,128,128]{2,1,0:T(8,128)S(1)}, s32[]{:T(128)}, f32[8,16]{1,0:T(8,128)}, f32[8,16,128,128]{3,2,1,0:T(8,128)}, /*index=5*/s32[]{:T(128)}, s32[]{:T(128)}) while((s32[]{:T(128)}, f32[16,128,128]{2,1,0:T(8,128)S(1)}, s32[]{:T(128)}, f32[8,16]{1,0:T(8,128)}, f32[8,16,128,128]{3,2,1,0:T(8,128)}, ...), condition=%wide.region_3.4_spmd.clone, body=%wide.region_2.3_spmd.clone.sunk | while | flops 1048580 | bytes 3146025 | solution.py:57
  323.0 1.3 exponential_bitcast_fusion.2
  324.2 1.5 fusion.62
  325.7 1.3 exponential_bitcast_fusion.2
  326.9 1.5 fusion.62
  328.4 1.3 exponential_bitcast_fusion.2
  329.7 1.5 fusion.62
  331.1 1.3 exponential_bitcast_fusion.2
  332.4 1.5 fusion.62
  333.9 1.3 exponential_bitcast_fusion.2
  335.1 1.5 fusion.62
  336.6 1.3 exponential_bitcast_fusion.2
  337.9 1.5 fusion.62
  339.3 1.3 exponential_bitcast_fusion.2
  340.6 1.5 fusion.62
  342.1 1.3 fusion.1
  343.4 3.2 fusion.9
  346.7 1.6 copy.46
  348.3 0.3 mul.247
  348.7 7.3 %fusion.16 = f32[128,2048]{1,0:T(8,128)} fusion(bf16[2048,2048]{0,1:T(8,128)(2,1)} %bitcast.107, f32[16,8,16,128]{3,2,1,0:T(8,128)S(1)} %bitcast.110, f32[128,2048]{1,0:T(8,128)S(1)} %copy.46, f32[2048]{0:T(1024)S(1)} %copy-done.4, f32[2048]{0:T(1024)S(1)} %copy-done.2, bf16[128,2048]{1,0:T(8,128)(2,1)S(1)} %get-tuple-element.155), kind=kOutput, calls=%fused_computation.32 | convolution fusion | flops 1075314688 | bytes 12075008 | tf_op jit(solution)/shard_map/dot_general | solution.py:180
  356.0 12.3 %reduce-scatter.2.cloned.1.call-done = f32[128,1024]{1,0:T(8,128)} async-done(((f32[128,2048]{1,0:T(8,128)}), f32[128,1024]{1,0:T(8,128)}) %reduce-scatter.2.cloned.1.call-update) | async-done | bytes 524304 | tf_op jit(solution)/shard_map/reduce_scatter | solution.py:181
  368.3 1.1 add_convert_fusion
  369.4 3.1 collective-permute-start.1
  372.5 3.1 collective-permute-start.2
  375.6 0.7 fusion.53
  384.1 0.7 fusion.52
  384.7 1.3 collective-permute-done.2
  386.1 3.6 fusion.31
  (49 shorter events, 1.8 us)
Async XLA Ops:
  6.5 2.2 copy-start.7
  6.5 2.2 copy-start.1
  6.5 5.7 %copy-start = (bf16[128,1024]{1,0:T(8,128)(2,1)S(1)}, bf16[128,1024]{1,0:T(8,128)(2,1)}, u32[]{:S(2)}) copy-start(bf16[128,1024]{1,0:T(8,128)(2,1)} %param.17) | copy-start | bytes 786436
  6.5 9.5 %copy-start.6 = (f32[2048]{0:T(1024)S(1)}, f32[2048]{0:T(1024)}, u32[]{:S(2)}) copy-start(f32[2048]{0:T(1024)} %param.18) | copy-start | bytes 24580
  6.5 9.5 %copy-start.8 = (f32[16]{0:T(128)S(1)}, f32[16]{0:T(128)}, u32[]{:S(2)}) copy-start(f32[16]{0:T(128)} %param.22) | copy-start | bytes 196
  6.5 24.9 %all-gather.8.cloned.1.call-start = ((), (), s32[]{:S(2)}) async-start(), calls=%async_computation.2 | async-start | bytes 1572864 | tf_op jit(solution)/shard_map/all_gather | solution.py:130
  7.3 129.7 %all-gather.6.cloned.1.call-start = ((), (), s32[]{:S(2)}) async-start(), calls=%async_computation.1 | async-start | bytes 12582912 | tf_op jit(solution)/shard_map/all_gather | solution.py:129
  8.0 314.9 %all-gather.10.cloned.1.call-start = ((), (), s32[]{:S(2)}) async-start(), calls=%async_computation.4 | async-start | bytes 9437184 | tf_op jit(solution)/shard_map/all_gather | solution.py:48
  144.7 163.8 %copy-start.5 = (f32[16]{0:T(128)S(1)}, f32[16]{0:T(128)}, u32[]{:S(2)}) copy-start(f32[16]{0:T(128)} %param.24) | copy-start | bytes 196
  144.7 223.6 %reduce-scatter.2.cloned.1.call-start = ((), (), s32[]{:S(2)}) async-start(), calls=%async_computation.3 | async-start | bytes 1572864 | tf_op jit(solution)/shard_map/reduce_scatter | solution.py:181
  151.2 158.0 %collective-permute-start = (bf16[1,2048,1024]{1,2,0:T(8,128)(2,1)}, bf16[1,2048,1024]{1,2,0:T(8,128)(2,1)}, u32[]{:S(2)}, u32[]{:S(2)}) collective-permute-start(bf16[1,2048,1024]{1,2,0:T(8,128)(2,1)} %bitcast.108), channel_id=1, source_target_pairs={{0,2},{2,0},{1,3},{3,1},{4,6},{6,4},{5,7},{7,5},{8,10},{10,8},{9,1... | collective-permute-start | bytes 12582920 | tf_op jit(solution)/shard_map/ppermute | solution.py:29
  343.4 5.3 %copy-start.2 = (f32[2048]{0:T(1024)S(1)}, f32[2048]{0:T(1024)}, u32[]{:S(2)}) copy-start(f32[2048]{0:T(1024)} %broadcast_bitcast_fusion) | copy-start | bytes 24580
  343.4 5.3 %copy-start.4 = (f32[2048]{0:T(1024)S(1)}, f32[2048]{0:T(1024)}, u32[]{:S(2)}) copy-start(f32[2048]{0:T(1024)} %param.25) | copy-start | bytes 24580
  348.6 26.9 %copy-start.9 = (s32[1,4]{1,0:T(1,128)S(1)}, s32[1,4]{1,0:T(1,128)}, u32[]{:S(2)}) copy-start(s32[1,4]{1,0:T(1,128)} %param.28) | copy-start | bytes 52
  348.6 35.4 %copy-start.3 = (f32[1,4]{1,0:T(1,128)S(1)}, f32[1,4]{1,0:T(1,128)}, u32[]{:S(2)}) copy-start(f32[1,4]{1,0:T(1,128)} %param.29) | copy-start | bytes 52
  369.4 15.3 %collective-permute-start.1 = (bf16[128,1024]{1,0:T(8,128)(2,1)S(1)}, bf16[128,1024]{1,0:T(8,128)(2,1)S(1)}, u32[]{:S(2)}, u32[]{:S(2)}) collective-permute-start(bf16[128,1024]{1,0:T(8,128)(2,1)S(1)} %add_convert_fusion), channel_id=1, source_target_pairs={{0,2},{2,4},{4,6},{6,8},{8,10},{10,12},{12,14},{1,3},{3,5},{5,7},{... | collective-permute-start | bytes 786440 | tf_op jit(solution)/shard_map/ppermute | solution.py:68
  372.5 13.5 %collective-permute-start.2 = (bf16[128,1024]{1,0:T(8,128)(2,1)S(1)}, bf16[128,1024]{1,0:T(8,128)(2,1)S(1)}, u32[]{:S(2)}, u32[]{:S(2)}) collective-permute-start(bf16[128,1024]{1,0:T(8,128)(2,1)S(1)} %add_convert_fusion), channel_id=1, source_target_pairs={{2,0},{4,2},{6,4},{8,6},{10,8},{12,10},{14,12},{3,1},{5,3},{7,5},{... | collective-permute-start | bytes 786440 | tf_op jit(solution)/shard_map/ppermute | solution.py:70
Sparse Core Ops, SparseCore 0:
  8.9 22.4 all-gather.7
  33.0 104.0 all-gather.5
  144.8 172.1 all-gather.9
  356.1 12.1 reduce-scatter.1
